TPU v7x, 32 devices: a whole 2x2x4 slice. The times are simulated.
32 devices in a mesh: dp: 16 (over z, x, core), fsdp: 2 (over y).
Axes of the slice: x: 2, y: 2, z: 4, core: 2. Of those that a mesh axis runs over, the one named last changes fastest.
Arguments:
- picture_mean_embeddings: bfloat16 [640, 1152], P(('dp', 'fsdp')), may hold values from -0.1875 to 0.1875
- caption_tower_summary: bfloat16 [640, 1152], P(('dp', 'fsdp')), may hold values from -0.125 to 0.125
- caption_mapping_matrix: bfloat16 [1152, 1152], P('fsdp'), may hold values from -0.125 to 1
- picture_match_index: int32 [640], P('dp'), may hold values from 0 to 639, as said below
- sharpness_factor: float32 [1], replicated, may hold values from 40 to 56
- score_shift_term: float32 [1], replicated, may hold values from -11 to -10
Outputs:
- grad_image: float32 [640, 1152], P(('dp', 'fsdp'))
- grad_text: float32 [640, 1152], P(('dp', 'fsdp'))
- head_grad: float32 [1152, 1152], P('fsdp')
Inputs may be any that keep to these rules, and one draw needn't show every extreme that they name: `picture_match_index`: every text is the pair of exactly one image.
All inputs are finite; a program needn't handle non-finite values.
Results may differ from a plain program's by a relative error of at most 0.0086.
Values may be sent and summed in bfloat16 or wider, within the bound.
No kernel may reach another device: no remote copies, remote signals or barrier semaphores. Data moves between devices by JAX's collectives and lax.ppermute only.
A program may use at most 64 MiB of HBM per device.

v0:
```python
import jax
import jax.numpy as jnp
from jax import lax
from jax.sharding import PartitionSpec as P

epsilon = 1e-06


def passed_along(block, axis, distance):
    devices = range(lax.axis_size(axis))
    route = [((i - distance) % len(devices), i) for i in devices]
    return lax.ppermute(block, axis, route)


def normalize(values):
    norms = jnp.sqrt(jnp.sum(values * values, axis=1, keepdims=True) + epsilon)
    return (values / norms, norms)


def unproject(grad_unit, unit, norms):
    return (grad_unit - unit * jnp.sum(unit * grad_unit, axis=1, keepdims=True)) / norms


def per_device(
    picture_mean_embeddings,
    caption_tower_summary,
    caption_mapping_matrix,
    picture_match_index,
    sharpness_factor,
    score_shift_term,
):
    rows = caption_tower_summary.shape[0]
    width = caption_mapping_matrix.shape[1]
    cycle_size = lax.axis_size("dp")
    column_count = lax.axis_size("fsdp")
    cycle_index = lax.axis_index("dp")
    column_index = lax.axis_index("fsdp")
    score_multiplier = sharpness_factor[0]
    offset = score_shift_term[0]
    feature_column_set = lax.all_to_all(
        caption_tower_summary, "fsdp", split_axis=1, concat_axis=0, tiled=True
    )
    projected = jnp.dot(
        caption_tower_summary,
        lax.all_gather(caption_mapping_matrix, "fsdp", axis=0, tiled=True),
        preferred_element_type=jnp.float32,
    )
    unit_text, text_norm = normalize(projected)
    text_unit = unit_text.astype(jnp.bfloat16)
    unit_image, image_norm = normalize(picture_mean_embeddings.astype(jnp.float32))
    image_unit = lax.all_gather(unit_image.astype(jnp.bfloat16), "fsdp", axis=0, tiled=True)
    group = image_unit.shape[0]

    def tile(block, text_rows):
        scores = lax.dot_general(
            image_unit, block, (((1,), (1,)), ((), ())), preferred_element_type=jnp.float32
        )
        logits = score_multiplier * scores + offset
        sign = jnp.where(picture_match_index[:, None] == text_rows[None, :], 1.0, -1.0).astype(
            jnp.float32
        )
        weights = (score_multiplier * -sign * jax.nn.sigmoid(-sign * logits)).astype(jnp.bfloat16)
        image_part = jnp.dot(weights, block, preferred_element_type=jnp.float32)
        text_part = lax.dot_general(
            weights, image_unit, (((0,), (0,)), ((), ())), preferred_element_type=jnp.float32
        )
        return (image_part, text_part)

    def rows_of(owner, count):
        return (owner * column_count + column_index) * rows + jnp.arange(count, dtype=jnp.int32)

    image_start = jnp.zeros((group, width), jnp.float32)

    def advance(count, state):
        block, carried, image_sum = state
        owner = (cycle_index - count) % cycle_size
        image_part, text_part = tile(block, rows_of(owner, rows))
        block = passed_along(block, "dp", 1)
        carried = passed_along(carried + text_part, "dp", 1)
        return (block, carried, image_sum + image_part)

    state = (text_unit, jnp.zeros((rows, width), jnp.float32), image_start)
    block, grad_zt, image_sum = lax.fori_loop(0, cycle_size, advance, state)
    grad_zi = lax.psum_scatter(image_sum, "fsdp", scatter_dimension=0, tiled=True)
    grad_image = unproject(grad_zi, unit_image, image_norm)
    grad_proj = unproject(grad_zt, unit_text, text_norm).astype(jnp.bfloat16)
    grad_group = lax.all_gather(grad_proj, "fsdp", axis=0, tiled=True)
    head_part = lax.dot_general(
        feature_column_set, grad_group, (((0,), (0,)), ((), ())), preferred_element_type=jnp.float32
    )
    head_grad = lax.psum(head_part, "dp")
    grad_text = lax.dot_general(
        grad_proj,
        lax.all_gather(caption_mapping_matrix, "fsdp", axis=0, tiled=True),
        (((1,), (1,)), ((), ())),
        preferred_element_type=jnp.float32,
    )
    return (grad_image, grad_text, head_grad)


def solution(mesh):
    return jax.shard_map(
        per_device,
        mesh=mesh,
        in_specs=(
            P(("dp", "fsdp"), None),
            P(("dp", "fsdp"), None),
            P("fsdp", None),
            P("dp"),
            P(),
            P(),
        ),
        out_specs=(P(("dp", "fsdp"), None), P(("dp", "fsdp"), None), P("fsdp", None)),
        check_vma=False,
    )
```

profile of v0, /device:TPU:0, one launch (start us, length us, event | category | flops | bytes accessed | tf_op | source)
XLA Modules:
  0.0 326.0 jit_solution(13299406759455780715)
XLA Ops:
  7.9 0.9 all_to_all.14
  9.5 4.2 %all-to-all-start = ((bf16[20,2,576]{2,0,1:T(8,128)(2,1)}), bf16[20,2,576]{2,0,1:T(8,128)(2,1)S(1)}, u32[]{:S(2)}, u32[]{:S(2)}) async-start(bf16[20,2,576]{2,0,1:T(8,128)(2,1)} %copy.10), calls=%async_computation | async-start | bytes 122880 | tf_op jit(solution)/shard_map/all_to_all | solution.py:40
  13.7 0.9 fusion.8
  15.6 4.9 %all-gather = bf16[2,20,1152]{2,1,0:T(8,128)(2,1)S(1)} all-gather(bf16[1,20,1152]{2,1,0:T(8,128)(2,1)S(1)} %convert_bitcast_fusion), channel_id=1, replica_groups=mesh['dp'=16,'fsdp'=2] {'fsdp'}, dimensions={0}, use_global_device_ids=true | all-gather | bytes 138240 | tf_op jit(solution)/shard_map/all_gather | solution.py:51
  20.5 31.2 %all-gather.4.cloned.1.call-done = bf16[1152,1152]{1,0:T(8,128)(2,1)} async-done(((bf16[576,1152]{1,0:T(8,128)(2,1)}), bf16[1152,1152]{1,0:T(8,128)(2,1)}) %all-gather.4.cloned.1.call-update) | async-done | bytes 2654224 | tf_op jit(solution)/shard_map/all_gather | solution.py:45
  51.7 2.4 multiply_reduce_fusion.2
  54.2 137.5 %while.20 = (s32[]{:T(128)}, bf16[20,1152]{1,0:T(8,128)(2,1)S(1)}, f32[20,1152]{1,0:T(8,128)S(1)}, f32[40,1152]{1,0:T(8,128)S(1)}, f32[]{:T(128)}, /*index=5*/s3...) while((s32[]{:T(128)}, bf16[20,1152]{1,0:T(8,128)(2,1)S(1)}, ...), condition=%wide.region_3.4_spmd.clone, body=%wide.region_2.3_spmd.clone.sunk | while | flops 5654438 | bytes 1480088 | solution.py:83
  54.3 1.5 fusion.36
  55.9 1.6 collective-permute-start.1
  57.8 2.8 collective-permute-done
  60.5 2.3 collective-permute-done.1
  62.9 1.5 fusion.36
  64.8 4.3 %collective-permute-done = bf16[20,1152]{1,0:T(8,128)(2,1)S(1)} collective-permute-done((bf16[20,1152]{1,0:T(8,128)(2,1)S(1)}, bf16[20,1152]{1,0:T(8,128)(2,1)S(1)}, u32[]{:S(2)}, u32[]{:S(2)}) %collective-permute-start) | collective-permute-done | bytes 46112 | tf_op jit(solution)/shard_map/while/body/eval_jaxpr/ppermute | solution.py:12
  69.1 2.3 collective-permute-done.1
  71.5 1.5 fusion.36
  73.4 4.3 %collective-permute-done = bf16[20,1152]{1,0:T(8,128)(2,1)S(1)} collective-permute-done((bf16[20,1152]{1,0:T(8,128)(2,1)S(1)}, bf16[20,1152]{1,0:T(8,128)(2,1)S(1)}, u32[]{:S(2)}, u32[]{:S(2)}) %collective-permute-start) | collective-permute-done | bytes 46112 | tf_op jit(solution)/shard_map/while/body/eval_jaxpr/ppermute | solution.py:12
  77.7 2.3 collective-permute-done.1
  80.1 1.5 fusion.36
  82.0 4.3 %collective-permute-done = bf16[20,1152]{1,0:T(8,128)(2,1)S(1)} collective-permute-done((bf16[20,1152]{1,0:T(8,128)(2,1)S(1)}, bf16[20,1152]{1,0:T(8,128)(2,1)S(1)}, u32[]{:S(2)}, u32[]{:S(2)}) %collective-permute-start) | collective-permute-done | bytes 46112 | tf_op jit(solution)/shard_map/while/body/eval_jaxpr/ppermute | solution.py:12
  86.3 2.3 collective-permute-done.1
  88.7 1.5 fusion.36
  90.6 4.3 %collective-permute-done = bf16[20,1152]{1,0:T(8,128)(2,1)S(1)} collective-permute-done((bf16[20,1152]{1,0:T(8,128)(2,1)S(1)}, bf16[20,1152]{1,0:T(8,128)(2,1)S(1)}, u32[]{:S(2)}, u32[]{:S(2)}) %collective-permute-start) | collective-permute-done | bytes 46112 | tf_op jit(solution)/shard_map/while/body/eval_jaxpr/ppermute | solution.py:12
  94.9 2.3 collective-permute-done.1
  97.3 1.5 fusion.36
  99.2 4.3 %collective-permute-done = bf16[20,1152]{1,0:T(8,128)(2,1)S(1)} collective-permute-done((bf16[20,1152]{1,0:T(8,128)(2,1)S(1)}, bf16[20,1152]{1,0:T(8,128)(2,1)S(1)}, u32[]{:S(2)}, u32[]{:S(2)}) %collective-permute-start) | collective-permute-done | bytes 46112 | tf_op jit(solution)/shard_map/while/body/eval_jaxpr/ppermute | solution.py:12
  103.5 2.3 collective-permute-done.1
  105.8 1.5 fusion.36
  107.8 4.3 %collective-permute-done = bf16[20,1152]{1,0:T(8,128)(2,1)S(1)} collective-permute-done((bf16[20,1152]{1,0:T(8,128)(2,1)S(1)}, bf16[20,1152]{1,0:T(8,128)(2,1)S(1)}, u32[]{:S(2)}, u32[]{:S(2)}) %collective-permute-start) | collective-permute-done | bytes 46112 | tf_op jit(solution)/shard_map/while/body/eval_jaxpr/ppermute | solution.py:12
  112.1 2.3 collective-permute-done.1
  114.4 1.5 fusion.36
  116.4 4.3 %collective-permute-done = bf16[20,1152]{1,0:T(8,128)(2,1)S(1)} collective-permute-done((bf16[20,1152]{1,0:T(8,128)(2,1)S(1)}, bf16[20,1152]{1,0:T(8,128)(2,1)S(1)}, u32[]{:S(2)}, u32[]{:S(2)}) %collective-permute-start) | collective-permute-done | bytes 46112 | tf_op jit(solution)/shard_map/while/body/eval_jaxpr/ppermute | solution.py:12
  120.7 2.3 collective-permute-done.1
  123.0 1.5 fusion.36
  124.9 4.3 %collective-permute-done = bf16[20,1152]{1,0:T(8,128)(2,1)S(1)} collective-permute-done((bf16[20,1152]{1,0:T(8,128)(2,1)S(1)}, bf16[20,1152]{1,0:T(8,128)(2,1)S(1)}, u32[]{:S(2)}, u32[]{:S(2)}) %collective-permute-start) | collective-permute-done | bytes 46112 | tf_op jit(solution)/shard_map/while/body/eval_jaxpr/ppermute | solution.py:12
  129.3 2.3 collective-permute-done.1
  131.6 1.5 fusion.36
  133.5 4.3 %collective-permute-done = bf16[20,1152]{1,0:T(8,128)(2,1)S(1)} collective-permute-done((bf16[20,1152]{1,0:T(8,128)(2,1)S(1)}, bf16[20,1152]{1,0:T(8,128)(2,1)S(1)}, u32[]{:S(2)}, u32[]{:S(2)}) %collective-permute-start) | collective-permute-done | bytes 46112 | tf_op jit(solution)/shard_map/while/body/eval_jaxpr/ppermute | solution.py:12
  137.8 2.3 collective-permute-done.1
  140.2 1.5 fusion.36
  142.1 4.3 %collective-permute-done = bf16[20,1152]{1,0:T(8,128)(2,1)S(1)} collective-permute-done((bf16[20,1152]{1,0:T(8,128)(2,1)S(1)}, bf16[20,1152]{1,0:T(8,128)(2,1)S(1)}, u32[]{:S(2)}, u32[]{:S(2)}) %collective-permute-start) | collective-permute-done | bytes 46112 | tf_op jit(solution)/shard_map/while/body/eval_jaxpr/ppermute | solution.py:12
  146.4 2.3 collective-permute-done.1
  148.8 1.5 fusion.36
  150.7 4.3 %collective-permute-done = bf16[20,1152]{1,0:T(8,128)(2,1)S(1)} collective-permute-done((bf16[20,1152]{1,0:T(8,128)(2,1)S(1)}, bf16[20,1152]{1,0:T(8,128)(2,1)S(1)}, u32[]{:S(2)}, u32[]{:S(2)}) %collective-permute-start) | collective-permute-done | bytes 46112 | tf_op jit(solution)/shard_map/while/body/eval_jaxpr/ppermute | solution.py:12
  155.0 2.3 collective-permute-done.1
  157.4 1.5 fusion.36
  159.3 4.3 %collective-permute-done = bf16[20,1152]{1,0:T(8,128)(2,1)S(1)} collective-permute-done((bf16[20,1152]{1,0:T(8,128)(2,1)S(1)}, bf16[20,1152]{1,0:T(8,128)(2,1)S(1)}, u32[]{:S(2)}, u32[]{:S(2)}) %collective-permute-start) | collective-permute-done | bytes 46112 | tf_op jit(solution)/shard_map/while/body/eval_jaxpr/ppermute | solution.py:12
  163.6 2.3 collective-permute-done.1
  166.0 1.5 fusion.36
  167.9 4.3 %collective-permute-done = bf16[20,1152]{1,0:T(8,128)(2,1)S(1)} collective-permute-done((bf16[20,1152]{1,0:T(8,128)(2,1)S(1)}, bf16[20,1152]{1,0:T(8,128)(2,1)S(1)}, u32[]{:S(2)}, u32[]{:S(2)}) %collective-permute-start) | collective-permute-done | bytes 46112 | tf_op jit(solution)/shard_map/while/body/eval_jaxpr/ppermute | solution.py:12
  172.2 2.3 collective-permute-done.1
  174.5 1.5 fusion.36
  176.5 4.3 %collective-permute-done = bf16[20,1152]{1,0:T(8,128)(2,1)S(1)} collective-permute-done((bf16[20,1152]{1,0:T(8,128)(2,1)S(1)}, bf16[20,1152]{1,0:T(8,128)(2,1)S(1)}, u32[]{:S(2)}, u32[]{:S(2)}) %collective-permute-start) | collective-permute-done | bytes 46112 | tf_op jit(solution)/shard_map/while/body/eval_jaxpr/ppermute | solution.py:12
  180.8 2.3 collective-permute-done.1
  183.1 1.5 fusion.36
  185.1 4.3 %collective-permute-done = bf16[20,1152]{1,0:T(8,128)(2,1)S(1)} collective-permute-done((bf16[20,1152]{1,0:T(8,128)(2,1)S(1)}, bf16[20,1152]{1,0:T(8,128)(2,1)S(1)}, u32[]{:S(2)}, u32[]{:S(2)}) %collective-permute-start) | collective-permute-done | bytes 46112 | tf_op jit(solution)/shard_map/while/body/eval_jaxpr/ppermute | solution.py:12
  189.4 2.3 collective-permute-done.1
  192.7 5.7 %all-gather.1 = bf16[2,20,1152]{2,1,0:T(8,128)(2,1)S(1)} all-gather(bf16[1,20,1152]{2,1,0:T(8,128)(2,1)S(1)} %bitcast.33), channel_id=1, replica_groups=mesh['dp'=16,'fsdp'=2] {'fsdp'}, dimensions={0}, use_global_device_ids=true | all-gather | bytes 138240 | tf_op jit(solution)/shard_map/all_gather | solution.py:87
  198.5 2.1 convolution_bitcast_fusion
  201.8 1.5 fusion.10
  203.4 7.5 %all-reduce.6.cloned.1.call-done = f32[40,1152]{1,0:T(8,128)} async-done(((f32[40,1152]{1,0:T(8,128)}), f32[40,1152]{1,0:T(8,128)}) %all-reduce.6.cloned.1.call-update) | async-done | bytes 184336
  210.8 1.1 multiply_reduce_fusion.1
  211.9 1.7 subtract_divide_fusion
  213.6 102.4 %all-reduce.4.cloned.1.call-done = f32[576,1152]{1,0:T(8,128)} async-done(((f32[576,1152]{1,0:T(8,128)}), f32[576,1152]{1,0:T(8,128)}) %all-reduce.4.cloned.1.call-update) | async-done | bytes 2654224 | tf_op jit(solution)/shard_map/psum | solution.py:91
  316.0 3.4 %copy.25 = f32[576,1152]{1,0:T(8,128)} copy(f32[576,1152]{1,0:T(8,128)} %all-reduce.4.cloned.1.call-done) | data formatting | bytes 5308416
  (125 shorter events, 11.2 us)
Async XLA Ops:
  7.2 47.0 %copy-start.3 = (s32[40]{0:T(128)S(1)}, s32[40]{0:T(128)}, u32[]{:S(2)}) copy-start(s32[40]{0:T(128)} %param.11) | copy-start | bytes 484
  7.2 44.5 %all-gather.4.cloned.1.call-start = ((), (), s32[]{:S(2)}) async-start(), calls=%async_computation.1 | async-start | bytes 3981312 | tf_op jit(solution)/shard_map/all_gather | solution.py:45
  9.5 11.0 %all-to-all-start = ((bf16[20,2,576]{2,0,1:T(8,128)(2,1)}), bf16[20,2,576]{2,0,1:T(8,128)(2,1)S(1)}, u32[]{:S(2)}, u32[]{:S(2)}) async-start(bf16[20,2,576]{2,0,1:T(8,128)(2,1)} %copy.10), calls=%async_computation | async-start | bytes 122880 | tf_op jit(solution)/shard_map/all_to_all | solution.py:40
  13.7 197.1 %all-reduce.6.cloned.1.call-start = ((), (), s32[]{:S(2)}) async-start(), calls=%async_computation.3 | async-start | bytes 368640
  54.2 6.3 %collective-permute-start = (bf16[20,1152]{1,0:T(8,128)(2,1)S(1)}, bf16[20,1152]{1,0:T(8,128)(2,1)S(1)}, u32[]{:S(2)}, u32[]{:S(2)}) collective-permute-start(bf16[20,1152]{1,0:T(8,128)(2,1)S(1)} %copy.16), channel_id=1, source_target_pairs={{30,0},{0,2},{2,4},{4,6},{6,8},{8,10},{10,12},{12,14},{14,16},{16,... | collective-permute-start | bytes 138248 | tf_op jit(solution)/shard_map/while/body/eval_jaxpr/ppermute | solution.py:12
  55.9 6.9 %collective-permute-start.1 = (f32[20,1152]{1,0:T(8,128)S(1)}, f32[20,1152]{1,0:T(8,128)S(1)}, u32[]{:S(2)}, u32[]{:S(2)}) collective-permute-start(f32[20,1152]{1,0:T(8,128)S(1)} %convolution_add_fusion.4), channel_id=1, source_target_pairs={{30,0},{0,2},{2,4},{4,6},{6,8},{8,10},{10,12},{12,14},{14,16},{16,... | collective-permute-start | bytes 276488 | tf_op jit(solution)/shard_map/while/body/eval_jaxpr/ppermute | solution.py:12
  62.9 6.3 %collective-permute-start = (bf16[20,1152]{1,0:T(8,128)(2,1)S(1)}, bf16[20,1152]{1,0:T(8,128)(2,1)S(1)}, u32[]{:S(2)}, u32[]{:S(2)}) collective-permute-start(bf16[20,1152]{1,0:T(8,128)(2,1)S(1)} %copy.16), channel_id=1, source_target_pairs={{30,0},{0,2},{2,4},{4,6},{6,8},{8,10},{10,12},{12,14},{14,16},{16,... | collective-permute-start | bytes 138248 | tf_op jit(solution)/shard_map/while/body/eval_jaxpr/ppermute | solution.py:12
  64.5 6.9 %collective-permute-start.1 = (f32[20,1152]{1,0:T(8,128)S(1)}, f32[20,1152]{1,0:T(8,128)S(1)}, u32[]{:S(2)}, u32[]{:S(2)}) collective-permute-start(f32[20,1152]{1,0:T(8,128)S(1)} %convolution_add_fusion.4), channel_id=1, source_target_pairs={{30,0},{0,2},{2,4},{4,6},{6,8},{8,10},{10,12},{12,14},{14,16},{16,... | collective-permute-start | bytes 276488 | tf_op jit(solution)/shard_map/while/body/eval_jaxpr/ppermute | solution.py:12
  71.4 6.3 %collective-permute-start = (bf16[20,1152]{1,0:T(8,128)(2,1)S(1)}, bf16[20,1152]{1,0:T(8,128)(2,1)S(1)}, u32[]{:S(2)}, u32[]{:S(2)}) collective-permute-start(bf16[20,1152]{1,0:T(8,128)(2,1)S(1)} %copy.16), channel_id=1, source_target_pairs={{30,0},{0,2},{2,4},{4,6},{6,8},{8,10},{10,12},{12,14},{14,16},{16,... | collective-permute-start | bytes 138248 | tf_op jit(solution)/shard_map/while/body/eval_jaxpr/ppermute | solution.py:12
  73.1 6.9 %collective-permute-start.1 = (f32[20,1152]{1,0:T(8,128)S(1)}, f32[20,1152]{1,0:T(8,128)S(1)}, u32[]{:S(2)}, u32[]{:S(2)}) collective-permute-start(f32[20,1152]{1,0:T(8,128)S(1)} %convolution_add_fusion.4), channel_id=1, source_target_pairs={{30,0},{0,2},{2,4},{4,6},{6,8},{8,10},{10,12},{12,14},{14,16},{16,... | collective-permute-start | bytes 276488 | tf_op jit(solution)/shard_map/while/body/eval_jaxpr/ppermute | solution.py:12
  80.0 6.3 %collective-permute-start = (bf16[20,1152]{1,0:T(8,128)(2,1)S(1)}, bf16[20,1152]{1,0:T(8,128)(2,1)S(1)}, u32[]{:S(2)}, u32[]{:S(2)}) collective-permute-start(bf16[20,1152]{1,0:T(8,128)(2,1)S(1)} %copy.16), channel_id=1, source_target_pairs={{30,0},{0,2},{2,4},{4,6},{6,8},{8,10},{10,12},{12,14},{14,16},{16,... | collective-permute-start | bytes 138248 | tf_op jit(solution)/shard_map/while/body/eval_jaxpr/ppermute | solution.py:12
  81.7 6.9 %collective-permute-start.1 = (f32[20,1152]{1,0:T(8,128)S(1)}, f32[20,1152]{1,0:T(8,128)S(1)}, u32[]{:S(2)}, u32[]{:S(2)}) collective-permute-start(f32[20,1152]{1,0:T(8,128)S(1)} %convolution_add_fusion.4), channel_id=1, source_target_pairs={{30,0},{0,2},{2,4},{4,6},{6,8},{8,10},{10,12},{12,14},{14,16},{16,... | collective-permute-start | bytes 276488 | tf_op jit(solution)/shard_map/while/body/eval_jaxpr/ppermute | solution.py:12
  88.6 6.3 %collective-permute-start = (bf16[20,1152]{1,0:T(8,128)(2,1)S(1)}, bf16[20,1152]{1,0:T(8,128)(2,1)S(1)}, u32[]{:S(2)}, u32[]{:S(2)}) collective-permute-start(bf16[20,1152]{1,0:T(8,128)(2,1)S(1)} %copy.16), channel_id=1, source_target_pairs={{30,0},{0,2},{2,4},{4,6},{6,8},{8,10},{10,12},{12,14},{14,16},{16,... | collective-permute-start | bytes 138248 | tf_op jit(solution)/shard_map/while/body/eval_jaxpr/ppermute | solution.py:12
  90.3 6.9 %collective-permute-start.1 = (f32[20,1152]{1,0:T(8,128)S(1)}, f32[20,1152]{1,0:T(8,128)S(1)}, u32[]{:S(2)}, u32[]{:S(2)}) collective-permute-start(f32[20,1152]{1,0:T(8,128)S(1)} %convolution_add_fusion.4), channel_id=1, source_target_pairs={{30,0},{0,2},{2,4},{4,6},{6,8},{8,10},{10,12},{12,14},{14,16},{16,... | collective-permute-start | bytes 276488 | tf_op jit(solution)/shard_map/while/body/eval_jaxpr/ppermute | solution.py:12
  97.2 6.3 %collective-permute-start = (bf16[20,1152]{1,0:T(8,128)(2,1)S(1)}, bf16[20,1152]{1,0:T(8,128)(2,1)S(1)}, u32[]{:S(2)}, u32[]{:S(2)}) collective-permute-start(bf16[20,1152]{1,0:T(8,128)(2,1)S(1)} %copy.16), channel_id=1, source_target_pairs={{30,0},{0,2},{2,4},{4,6},{6,8},{8,10},{10,12},{12,14},{14,16},{16,... | collective-permute-start | bytes 138248 | tf_op jit(solution)/shard_map/while/body/eval_jaxpr/ppermute | solution.py:12
  98.9 6.9 %collective-permute-start.1 = (f32[20,1152]{1,0:T(8,128)S(1)}, f32[20,1152]{1,0:T(8,128)S(1)}, u32[]{:S(2)}, u32[]{:S(2)}) collective-permute-start(f32[20,1152]{1,0:T(8,128)S(1)} %convolution_add_fusion.4), channel_id=1, source_target_pairs={{30,0},{0,2},{2,4},{4,6},{6,8},{8,10},{10,12},{12,14},{14,16},{16,... | collective-permute-start | bytes 276488 | tf_op jit(solution)/shard_map/while/body/eval_jaxpr/ppermute | solution.py:12
  105.8 6.3 %collective-permute-start = (bf16[20,1152]{1,0:T(8,128)(2,1)S(1)}, bf16[20,1152]{1,0:T(8,128)(2,1)S(1)}, u32[]{:S(2)}, u32[]{:S(2)}) collective-permute-start(bf16[20,1152]{1,0:T(8,128)(2,1)S(1)} %copy.16), channel_id=1, source_target_pairs={{30,0},{0,2},{2,4},{4,6},{6,8},{8,10},{10,12},{12,14},{14,16},{16,... | collective-permute-start | bytes 138248 | tf_op jit(solution)/shard_map/while/body/eval_jaxpr/ppermute | solution.py:12
  107.5 6.9 %collective-permute-start.1 = (f32[20,1152]{1,0:T(8,128)S(1)}, f32[20,1152]{1,0:T(8,128)S(1)}, u32[]{:S(2)}, u32[]{:S(2)}) collective-permute-start(f32[20,1152]{1,0:T(8,128)S(1)} %convolution_add_fusion.4), channel_id=1, source_target_pairs={{30,0},{0,2},{2,4},{4,6},{6,8},{8,10},{10,12},{12,14},{14,16},{16,... | collective-permute-start | bytes 276488 | tf_op jit(solution)/shard_map/while/body/eval_jaxpr/ppermute | solution.py:12
  114.4 6.3 %collective-permute-start = (bf16[20,1152]{1,0:T(8,128)(2,1)S(1)}, bf16[20,1152]{1,0:T(8,128)(2,1)S(1)}, u32[]{:S(2)}, u32[]{:S(2)}) collective-permute-start(bf16[20,1152]{1,0:T(8,128)(2,1)S(1)} %copy.16), channel_id=1, source_target_pairs={{30,0},{0,2},{2,4},{4,6},{6,8},{8,10},{10,12},{12,14},{14,16},{16,... | collective-permute-start | bytes 138248 | tf_op jit(solution)/shard_map/while/body/eval_jaxpr/ppermute | solution.py:12
  116.0 6.9 %collective-permute-start.1 = (f32[20,1152]{1,0:T(8,128)S(1)}, f32[20,1152]{1,0:T(8,128)S(1)}, u32[]{:S(2)}, u32[]{:S(2)}) collective-permute-start(f32[20,1152]{1,0:T(8,128)S(1)} %convolution_add_fusion.4), channel_id=1, source_target_pairs={{30,0},{0,2},{2,4},{4,6},{6,8},{8,10},{10,12},{12,14},{14,16},{16,... | collective-permute-start | bytes 276488 | tf_op jit(solution)/shard_map/while/body/eval_jaxpr/ppermute | solution.py:12
  123.0 6.3 %collective-permute-start = (bf16[20,1152]{1,0:T(8,128)(2,1)S(1)}, bf16[20,1152]{1,0:T(8,128)(2,1)S(1)}, u32[]{:S(2)}, u32[]{:S(2)}) collective-permute-start(bf16[20,1152]{1,0:T(8,128)(2,1)S(1)} %copy.16), channel_id=1, source_target_pairs={{30,0},{0,2},{2,4},{4,6},{6,8},{8,10},{10,12},{12,14},{14,16},{16,... | collective-permute-start | bytes 138248 | tf_op jit(solution)/shard_map/while/body/eval_jaxpr/ppermute | solution.py:12
  124.6 6.9 %collective-permute-start.1 = (f32[20,1152]{1,0:T(8,128)S(1)}, f32[20,1152]{1,0:T(8,128)S(1)}, u32[]{:S(2)}, u32[]{:S(2)}) collective-permute-start(f32[20,1152]{1,0:T(8,128)S(1)} %convolution_add_fusion.4), channel_id=1, source_target_pairs={{30,0},{0,2},{2,4},{4,6},{6,8},{8,10},{10,12},{12,14},{14,16},{16,... | collective-permute-start | bytes 276488 | tf_op jit(solution)/shard_map/while/body/eval_jaxpr/ppermute | solution.py:12
  131.6 6.3 %collective-permute-start = (bf16[20,1152]{1,0:T(8,128)(2,1)S(1)}, bf16[20,1152]{1,0:T(8,128)(2,1)S(1)}, u32[]{:S(2)}, u32[]{:S(2)}) collective-permute-start(bf16[20,1152]{1,0:T(8,128)(2,1)S(1)} %copy.16), channel_id=1, source_target_pairs={{30,0},{0,2},{2,4},{4,6},{6,8},{8,10},{10,12},{12,14},{14,16},{16,... | collective-permute-start | bytes 138248 | tf_op jit(solution)/shard_map/while/body/eval_jaxpr/ppermute | solution.py:12
  133.2 6.9 %collective-permute-start.1 = (f32[20,1152]{1,0:T(8,128)S(1)}, f32[20,1152]{1,0:T(8,128)S(1)}, u32[]{:S(2)}, u32[]{:S(2)}) collective-permute-start(f32[20,1152]{1,0:T(8,128)S(1)} %convolution_add_fusion.4), channel_id=1, source_target_pairs={{30,0},{0,2},{2,4},{4,6},{6,8},{8,10},{10,12},{12,14},{14,16},{16,... | collective-permute-start | bytes 276488 | tf_op jit(solution)/shard_map/while/body/eval_jaxpr/ppermute | solution.py:12
  140.1 6.3 %collective-permute-start = (bf16[20,1152]{1,0:T(8,128)(2,1)S(1)}, bf16[20,1152]{1,0:T(8,128)(2,1)S(1)}, u32[]{:S(2)}, u32[]{:S(2)}) collective-permute-start(bf16[20,1152]{1,0:T(8,128)(2,1)S(1)} %copy.16), channel_id=1, source_target_pairs={{30,0},{0,2},{2,4},{4,6},{6,8},{8,10},{10,12},{12,14},{14,16},{16,... | collective-permute-start | bytes 138248 | tf_op jit(solution)/shard_map/while/body/eval_jaxpr/ppermute | solution.py:12
  141.8 6.9 %collective-permute-start.1 = (f32[20,1152]{1,0:T(8,128)S(1)}, f32[20,1152]{1,0:T(8,128)S(1)}, u32[]{:S(2)}, u32[]{:S(2)}) collective-permute-start(f32[20,1152]{1,0:T(8,128)S(1)} %convolution_add_fusion.4), channel_id=1, source_target_pairs={{30,0},{0,2},{2,4},{4,6},{6,8},{8,10},{10,12},{12,14},{14,16},{16,... | collective-permute-start | bytes 276488 | tf_op jit(solution)/shard_map/while/body/eval_jaxpr/ppermute | solution.py:12
  148.7 6.3 %collective-permute-start = (bf16[20,1152]{1,0:T(8,128)(2,1)S(1)}, bf16[20,1152]{1,0:T(8,128)(2,1)S(1)}, u32[]{:S(2)}, u32[]{:S(2)}) collective-permute-start(bf16[20,1152]{1,0:T(8,128)(2,1)S(1)} %copy.16), channel_id=1, source_target_pairs={{30,0},{0,2},{2,4},{4,6},{6,8},{8,10},{10,12},{12,14},{14,16},{16,... | collective-permute-start | bytes 138248 | tf_op jit(solution)/shard_map/while/body/eval_jaxpr/ppermute | solution.py:12
  150.4 6.9 %collective-permute-start.1 = (f32[20,1152]{1,0:T(8,128)S(1)}, f32[20,1152]{1,0:T(8,128)S(1)}, u32[]{:S(2)}, u32[]{:S(2)}) collective-permute-start(f32[20,1152]{1,0:T(8,128)S(1)} %convolution_add_fusion.4), channel_id=1, source_target_pairs={{30,0},{0,2},{2,4},{4,6},{6,8},{8,10},{10,12},{12,14},{14,16},{16,... | collective-permute-start | bytes 276488 | tf_op jit(solution)/shard_map/while/body/eval_jaxpr/ppermute | solution.py:12
  157.3 6.3 %collective-permute-start = (bf16[20,1152]{1,0:T(8,128)(2,1)S(1)}, bf16[20,1152]{1,0:T(8,128)(2,1)S(1)}, u32[]{:S(2)}, u32[]{:S(2)}) collective-permute-start(bf16[20,1152]{1,0:T(8,128)(2,1)S(1)} %copy.16), channel_id=1, source_target_pairs={{30,0},{0,2},{2,4},{4,6},{6,8},{8,10},{10,12},{12,14},{14,16},{16,... | collective-permute-start | bytes 138248 | tf_op jit(solution)/shard_map/while/body/eval_jaxpr/ppermute | solution.py:12
  159.0 6.9 %collective-permute-start.1 = (f32[20,1152]{1,0:T(8,128)S(1)}, f32[20,1152]{1,0:T(8,128)S(1)}, u32[]{:S(2)}, u32[]{:S(2)}) collective-permute-start(f32[20,1152]{1,0:T(8,128)S(1)} %convolution_add_fusion.4), channel_id=1, source_target_pairs={{30,0},{0,2},{2,4},{4,6},{6,8},{8,10},{10,12},{12,14},{14,16},{16,... | collective-permute-start | bytes 276488 | tf_op jit(solution)/shard_map/while/body/eval_jaxpr/ppermute | solution.py:12
  165.9 6.3 %collective-permute-start = (bf16[20,1152]{1,0:T(8,128)(2,1)S(1)}, bf16[20,1152]{1,0:T(8,128)(2,1)S(1)}, u32[]{:S(2)}, u32[]{:S(2)}) collective-permute-start(bf16[20,1152]{1,0:T(8,128)(2,1)S(1)} %copy.16), channel_id=1, source_target_pairs={{30,0},{0,2},{2,4},{4,6},{6,8},{8,10},{10,12},{12,14},{14,16},{16,... | collective-permute-start | bytes 138248 | tf_op jit(solution)/shard_map/while/body/eval_jaxpr/ppermute | solution.py:12
  167.6 6.9 %collective-permute-start.1 = (f32[20,1152]{1,0:T(8,128)S(1)}, f32[20,1152]{1,0:T(8,128)S(1)}, u32[]{:S(2)}, u32[]{:S(2)}) collective-permute-start(f32[20,1152]{1,0:T(8,128)S(1)} %convolution_add_fusion.4), channel_id=1, source_target_pairs={{30,0},{0,2},{2,4},{4,6},{6,8},{8,10},{10,12},{12,14},{14,16},{16,... | collective-permute-start | bytes 276488 | tf_op jit(solution)/shard_map/while/body/eval_jaxpr/ppermute | solution.py:12
  174.5 6.3 %collective-permute-start = (bf16[20,1152]{1,0:T(8,128)(2,1)S(1)}, bf16[20,1152]{1,0:T(8,128)(2,1)S(1)}, u32[]{:S(2)}, u32[]{:S(2)}) collective-permute-start(bf16[20,1152]{1,0:T(8,128)(2,1)S(1)} %copy.16), channel_id=1, source_target_pairs={{30,0},{0,2},{2,4},{4,6},{6,8},{8,10},{10,12},{12,14},{14,16},{16,... | collective-permute-start | bytes 138248 | tf_op jit(solution)/shard_map/while/body/eval_jaxpr/ppermute | solution.py:12
  176.2 6.9 %collective-permute-start.1 = (f32[20,1152]{1,0:T(8,128)S(1)}, f32[20,1152]{1,0:T(8,128)S(1)}, u32[]{:S(2)}, u32[]{:S(2)}) collective-permute-start(f32[20,1152]{1,0:T(8,128)S(1)} %convolution_add_fusion.4), channel_id=1, source_target_pairs={{30,0},{0,2},{2,4},{4,6},{6,8},{8,10},{10,12},{12,14},{14,16},{16,... | collective-permute-start | bytes 276488 | tf_op jit(solution)/shard_map/while/body/eval_jaxpr/ppermute | solution.py:12
  183.1 6.3 %collective-permute-start = (bf16[20,1152]{1,0:T(8,128)(2,1)S(1)}, bf16[20,1152]{1,0:T(8,128)(2,1)S(1)}, u32[]{:S(2)}, u32[]{:S(2)}) collective-permute-start(bf16[20,1152]{1,0:T(8,128)(2,1)S(1)} %copy.16), channel_id=1, source_target_pairs={{30,0},{0,2},{2,4},{4,6},{6,8},{8,10},{10,12},{12,14},{14,16},{16,... | collective-permute-start | bytes 138248 | tf_op jit(solution)/shard_map/while/body/eval_jaxpr/ppermute | solution.py:12
  184.7 6.9 %collective-permute-start.1 = (f32[20,1152]{1,0:T(8,128)S(1)}, f32[20,1152]{1,0:T(8,128)S(1)}, u32[]{:S(2)}, u32[]{:S(2)}) collective-permute-start(f32[20,1152]{1,0:T(8,128)S(1)} %convolution_add_fusion.4), channel_id=1, source_target_pairs={{30,0},{0,2},{2,4},{4,6},{6,8},{8,10},{10,12},{12,14},{14,16},{16,... | collective-permute-start | bytes 276488 | tf_op jit(solution)/shard_map/while/body/eval_jaxpr/ppermute | solution.py:12
  191.7 0.7 copy-start.1
  192.4 123.7 %all-reduce.4.cloned.1.call-start = ((), (), s32[]{:S(2)}) async-start(), calls=%async_computation.2 | async-start | bytes 5308416 | tf_op jit(solution)/shard_map/psum | solution.py:91
  198.4 2.1 copy-start.4
  198.5 3.3 %copy-start = (bf16[1152,1152]{1,0:T(8,128)(2,1)S(1)}, bf16[1152,1152]{1,0:T(8,128)(2,1)}, u32[]{:S(2)}) copy-start(bf16[1152,1152]{1,0:T(8,128)(2,1)} %all-gather.4.cloned.1.call-done) | copy-start | bytes 7962628
  200.5 10.3 %copy-start.2 = (bf16[20,1152]{1,0:T(8,128)(2,1)S(1)}, bf16[20,1152]{1,0:T(8,128)(2,1)}, u32[]{:S(2)}) copy-start(bf16[20,1152]{1,0:T(8,128)(2,1)} %param.8) | copy-start | bytes 138244
Sparse Core Ops, SparseCore 0:
  9.6 42.0 all-gather.3
  192.5 18.2 all-reduce.5
  215.0 100.9 all-reduce.3
where the time goes:
time: 327 us; the launch traced here: 326 us
  waiting for transfers between devices  246 us (75%)
  matrix products  35.2 us (11%)
  between operations  14.5 us (4%)
  blocking collectives  10.6 us (3%)
  starting transfers between devices  6.87 us (2%)
  local copies, waits for them, and re-layouts  6.44 us (2%)
  other arithmetic  5.06 us (2%)
    ppermute x32, waiting for transfers between devices, passed_along(): return lax.ppermute(block, axis, route)  104 us
    psum x1, waiting for transfers between devices, per_device(): head_grad = lax.psum(head_part, 'dp')  102 us
    all_gather x1, waiting for transfers between devices, per_device(): lax.all_gather(caption_mapping_matrix, 'fsdp', axis=0, tiled=True)  31.2 us
    dot_general x16, matrix products, tile(): lax.dot_general(image_unit, block, (((1,), (1,)), ((), ())), preferred_el...  23.3 us
    unnamed x4, waiting for transfers between devices  8.19 us
  transfers between devices with their start and end apart: 36, of which 35 were waited for; matrix products, arithmetic and copies ran while one was open for 12% of the time, Pallas kernels for 0%

commit v1 on v0

--- a/solution.py
+++ b/solution.py
@@ -1,6 +1,10 @@
+import functools
+
 import jax
 import jax.numpy as jnp
 from jax import lax
+from jax.experimental import pallas as pl
+from jax.experimental.pallas import tpu as pltpu
 from jax.sharding import PartitionSpec as P
 
 epsilon = 1e-06
@@ -21,7 +25,7 @@
     return (grad_unit - unit * jnp.sum(unit * grad_unit, axis=1, keepdims=True)) / norms
 
 
-def per_device(
+def ring_plan(
     picture_mean_embeddings,
     caption_tower_summary,
     caption_mapping_matrix,
@@ -98,7 +102,221 @@
     return (grad_image, grad_text, head_grad)
 
 
+def across(block, bits):
+    count = lax.axis_size("dp") * lax.axis_size("fsdp")
+    return lax.ppermute(block, ("dp", "fsdp"), [(i, i ^ bits) for i in range(count)])
+
+
+Y, CORE, X, Z1, Z2 = 1, 2, 4, 8, 16
+IMAGE_ORDER = (Y, X, Z2, Z1, CORE)
+TEXT_ORDER = (Y, Z2, Z1, X, CORE)
+NT = (((1,), (1,)), ((), ()))
+TN = (((0,), (0,)), ((), ()))
+
+
+def dot(a, b, dims=(((1,), (0,)), ((), ()))):
+    return lax.dot_general(a, b, dims, preferred_element_type=jnp.float32)
+
+
+def cuts(size, step):
+    return [slice(k, min(k + step, size)) for k in range(0, size, step)]
+
+
+def text_ids(shape, axis, rows, place):
+    row = lax.broadcasted_iota(jnp.int32, shape, axis)
+    block = sum((row >= k * rows).astype(jnp.int32) for k in range(1, shape[axis] // rows))
+    owner = jnp.zeros_like(row)
+    for k, bits in enumerate(TEXT_ORDER):
+        owner += ((block >> k) & 1) * bits
+    return (owner ^ place) * rows + row - block * rows
+
+
+def weigh(scores, paired, sharpness, shift):
+    logits = sharpness[0] * scores + shift[0]
+    sign = jnp.where(paired, 1.0, -1.0)
+    return (sharpness[0] * -sign * jax.nn.sigmoid(-sign * logits)).astype(jnp.bfloat16)
+
+
+def text_kernel(sharpness, shift, image, images, match, *rest):
+    (matrix_own, matrix_near, matrix_far), texts, rest = rest[:3], rest[3:7], rest[7:]
+    zt, projected, turned, matrix, grad_image, text, sems = rest
+    rows = image.shape[0]
+    total, width = text.shape
+    depth, near = matrix_own.shape[0], matrix_near.shape[0]
+    group, side = lax.axis_index("dp"), lax.axis_index("fsdp")
+    core = lax.rem(group, 2)
+
+    other = (1 - side) * depth
+    places = (side * depth, other + core * near, other + (1 - core) * near)
+    copies = []
+    for k, (source, start) in enumerate(zip((matrix_own, matrix_near, matrix_far), places)):
+        start = pl.multiple_of(start, 32)
+        target = matrix.at[pl.ds(start, source.shape[0])]
+        copies.append(pltpu.make_async_copy(source, target, sems.at[k]))
+        copies[-1].start()
+    count = total // len(texts)
+    for k, source in enumerate(texts):
+        text[pl.ds(k * count, count)] = source[...]
+    for s in (0, 1):
+
+        @pl.when(side == s)
+        def _():
+            turned[...] = jnp.transpose(text[:, s * depth : (s + 1) * depth])
+
+    for copy in copies:
+        copy.wait()
+
+    for cut in cuts(width, 256):
+        projected[:, cut] = dot(text[...], matrix[:, cut])
+    for block in cuts(total, 128):
+        value = projected[block]
+        inverse = lax.rsqrt(jnp.sum(value * value, axis=1, keepdims=True) + epsilon)
+        zt[block] = (value * inverse).astype(jnp.bfloat16)
+
+    scores = dot(images[...], zt[...], NT)
+    ids = text_ids((1, total), 1, rows, group * 2 + side)
+    weights = weigh(scores, match[...] == ids, sharpness, shift)
+    unit_image, image_norm = normalize(image[...].astype(jnp.float32))
+    grad_image[...] = unproject(dot(weights, zt[...])[:rows], unit_image, image_norm)
+
+
+def pair_kernel(rows, sharpness, shift, match, zt, projected, turned, matrix, *rest):
+    images, rest = rest[:4], rest[4:]
+    grad_text, head_grad, zi, weights, grad, proj, head, sems = rest
+    total, width = zi.shape
+    place = lax.axis_index("dp") * 2 + lax.axis_index("fsdp")
+    count = total // len(images)
+    for k, source in enumerate(images):
+        zi[pl.ds(k * count, count)] = source[...]
+
+    ids = text_ids((total, 1), 0, rows, place)
+    for cut in cuts(total, 256):
+        scores = dot(zt[...], zi[cut], NT)
+        weights[:, cut] = weigh(scores, ids == match[:, cut], sharpness, shift)
+    for cut in cuts(width, 256):
+        grad[:, cut] = dot(weights[...], zi[:, cut])
+    for block in cuts(total, 128):
+        value, slope = projected[block], grad[block]
+        squares = jnp.sum(value * value, axis=1, keepdims=True) + epsilon
+        inner = jnp.sum(value * slope, axis=1, keepdims=True)
+        proj[block] = ((slope - value * (inner / squares)) * lax.rsqrt(squares)).astype(
+            jnp.bfloat16
+        )
+    copies = []
+    for k, cut in enumerate(cuts(width, 256)):
+        head[:, cut] = dot(turned[...], proj[:, cut])
+        copies.append(pltpu.make_async_copy(head.at[:, cut], head_grad.at[:, cut], sems.at[k]))
+        copies[-1].start()
+    grad_text[...] = dot(proj[:48], matrix[...], NT)[:rows]
+    for copy in copies:
+        copy.wait()
+
+
+def gathered_plan(
+    picture_mean_embeddings,
+    caption_tower_summary,
+    caption_mapping_matrix,
+    picture_match_index,
+    sharpness_factor,
+    score_shift_term,
+):
+    rows, width = caption_tower_summary.shape
+    depth = caption_mapping_matrix.shape[0]
+    half = depth // 2
+    core = lax.axis_index("dp") % 2
+    side = lax.axis_index("fsdp")
+    total = rows * 32
+    smem = pl.BlockSpec(memory_space=pltpu.SMEM)
+    vmem = pl.BlockSpec(memory_space=pltpu.VMEM)
+    anywhere = pl.BlockSpec(memory_space=pl.ANY)
+    f32, bf16 = jnp.float32, jnp.bfloat16
+
+    def doubled(block, bits):
+        return jnp.concatenate([block, across(block, bits)])
+
+    texts = doubled(caption_tower_summary, TEXT_ORDER[0])
+    quarter = lax.dynamic_slice_in_dim(caption_mapping_matrix, core * half, half, 0)
+    quarter, _ = lax.optimization_barrier((quarter, texts))
+    near = across(quarter, Y)
+    far = across(near, CORE)
+    for bits in TEXT_ORDER[1:3]:
+        texts = doubled(texts, bits)
+    late = across(texts, TEXT_ORDER[3])
+    texts = [texts, late, across(texts, CORE), across(late, CORE)]
+
+    unit_image, _ = normalize(picture_mean_embeddings.astype(f32))
+    own_images = doubled(unit_image.astype(bf16), IMAGE_ORDER[0])
+    own_match = jnp.where(side == 0, picture_match_index, jnp.roll(picture_match_index, rows))
+    images, match = own_images, own_match
+    for bits in IMAGE_ORDER[1:3]:
+        match = doubled(match, bits)
+        images, match = lax.optimization_barrier((images, match))
+        images = doubled(images, bits)
+    match = doubled(match, IMAGE_ORDER[3])
+    images, match = lax.optimization_barrier((images, match))
+    late = across(images, IMAGE_ORDER[3])
+    match = doubled(match, CORE)
+    images = [images, late, across(images, CORE), across(late, CORE)]
+
+    zt, projected, turned, matrix, grad_image = pl.pallas_call(
+        text_kernel,
+        out_shape=(
+            jax.ShapeDtypeStruct((total, width), bf16),
+            jax.ShapeDtypeStruct((total, width), f32),
+            jax.ShapeDtypeStruct((depth, total), bf16),
+            jax.ShapeDtypeStruct((2 * depth, width), bf16),
+            jax.ShapeDtypeStruct((rows, width), f32),
+        ),
+        in_specs=[smem] * 2 + [vmem] * 3 + [anywhere] * 3 + [vmem] * 4,
+        out_specs=(vmem,) * 5,
+        scratch_shapes=[pltpu.VMEM((total, width), bf16), pltpu.SemaphoreType.DMA((3,))],
+        compiler_params=pltpu.CompilerParams(vmem_limit_bytes=24 * 2**20),
+        name="texts",
+    )(
+        sharpness_factor,
+        score_shift_term,
+        picture_mean_embeddings,
+        own_images,
+        own_match[:, None],
+        caption_mapping_matrix,
+        near,
+        far,
+        *texts,
+    )
+    grad_text, head_grad = pl.pallas_call(
+        functools.partial(pair_kernel, rows),
+        out_shape=(
+            jax.ShapeDtypeStruct((rows, width), f32),
+            jax.ShapeDtypeStruct((depth, width), f32),
+        ),
+        in_specs=[smem] * 2 + [vmem] * 9,
+        out_specs=(vmem, anywhere),
+        scratch_shapes=[
+            pltpu.VMEM((total, width), bf16),
+            pltpu.VMEM((total, total), bf16),
+            pltpu.VMEM((total, width), f32),
+            pltpu.VMEM((total, width), bf16),
+            pltpu.VMEM((depth, width), f32),
+            pltpu.SemaphoreType.DMA((8,)),
+        ],
+        compiler_params=pltpu.CompilerParams(vmem_limit_bytes=24 * 2**20),
+        name="pairs",
+    )(
+        sharpness_factor,
+        score_shift_term,
+        match[None, :],
+        zt,
+        projected,
+        turned,
+        matrix,
+        *images,
+    )
+    return (grad_image, grad_text, head_grad)
+
+
 def solution(mesh):
+    gathered = dict(mesh.shape) == {"dp": 16, "fsdp": 2}
+    per_device = gathered_plan if gathered else ring_plan
     return jax.shard_map(
         per_device,
         mesh=mesh,

time: 327 us -> 59.4 us (0.18)
  waiting for transfers between devices: 246 us -> 16.4 us
  matrix products: 35.2 us -> 0 us
  Pallas kernels: 0 us -> 14.5 us
  between operations: 14.5 us -> 2.06 us
  starting transfers between devices: 6.87 us -> 17.8 us
  blocking collectives: 10.6 us -> 0 us
    psum x1 -> x0, waiting for transfers between devices: 102 us -> none  [per_device(): head_grad = lax.psum(head_part, 'dp')]
    ppermute x32 -> x18, waiting for transfers between devices: 104 us -> 16.4 us  [across(): lax.ppermute(block, ('dp', 'fsdp'), [(i, i ^ bits) for i in range(count)])]
    dot_general x51 -> x0, matrix products: 35.2 us -> none  [the longest x16 23.3 us: tile(): lax.dot_general(image_unit, block, (((1,), (1,)), ((), ())), preferred_el...]
    all_gather x1 -> x0, waiting for transfers between devices: 31.2 us -> none  [per_device(): lax.all_gather(caption_mapping_matrix, 'fsdp', axis=0, tiled=True)]
    ppermute x32 -> x18, starting transfers between devices: 2.55 us -> 17.8 us  [across(): lax.ppermute(block, ('dp', 'fsdp'), [(i, i ^ bits) for i in range(count)])]
    pallas_call x0 -> x2, Pallas kernels: none -> 14.5 us  [the longest x1 7.87 us: gathered_plan(): pl.pallas_call(functools.partial(pair_kernel, rows), out_shape=(jax.Shape...]
    all_gather x2 -> x0, blocking collectives: 10.6 us -> none  [the longest x1 5.68 us: per_device(): grad_group = lax.all_gather(grad_proj, 'fsdp', axis=0, tiled=True)]
    unnamed x4 -> x0, waiting for transfers between devices: 8.19 us -> none
  transfers between devices with their start and end apart: 36 -> 18, of which waited for: 35 -> 7; matrix products, arithmetic and copies ran while one was open for 12% -> 9% of each run, Pallas kernels for 0% -> 11%
where the time goes in v1:
time: 59.4 us; the launch traced here: 58.9 us
  starting transfers between devices  17.8 us (30%)
  waiting for transfers between devices  16.4 us (28%)
  Pallas kernels  14.5 us (24%)
  other arithmetic  4.77 us (8%)
  local copies, waits for them, and re-layouts  3.38 us (6%)
  between operations  2.06 us (3%)
    ppermute x18, starting transfers between devices, across(): lax.ppermute(block, ('dp', 'fsdp'), [(i, i ^ bits) for i in range(count)])  17.8 us
    ppermute x18, waiting for transfers between devices, across(): lax.ppermute(block, ('dp', 'fsdp'), [(i, i ^ bits) for i in range(count)])  16.4 us
    pallas_call x1, Pallas kernels, gathered_plan(): pl.pallas_call(functools.partial(pair_kernel, rows), out_shape=(jax.Shape...  7.87 us
    pallas_call x1, Pallas kernels, gathered_plan(): pl.pallas_call(text_kernel, out_shape=(jax.ShapeDtypeStruct((total, width...  6.67 us
    concatenate x10, other arithmetic, doubled(): return jnp.concatenate([block, across(block, bits)])  2.08 us
  transfers between devices with their start and end apart: 18, of which 7 were waited for; matrix products, arithmetic and copies ran while one was open for 9% of the time, Pallas kernels for 11%

profile of v1, /device:TPU:0, one launch (start us, length us, event | category | flops | bytes accessed | tf_op | source)
XLA Modules:
  0.0 58.9 jit_solution(15899849623986522453)
XLA Ops:
  0.6 0.0 copy-start.1
  0.6 0.0 copy-start.3
  0.7 0.0 copy-start
  0.7 1.0 %fusion = f32[20]{0:T(128)S(1)} fusion(bf16[20,1152]{1,0:T(8,128)(2,1)} %image.1), kind=kLoop, calls=%fused_computation.6 | loop fusion | flops 69100 | bytes 46160 | tf_op jit(solution)/shard_map/reduce_sum | solution.py:20
  1.7 0.9 %fusion.1 = bf16[20,1152]{1,0:T(8,128)(2,1)S(1)} fusion(bf16[20,1152]{1,0:T(8,128)(2,1)} %image.1, f32[20]{0:T(128)S(1)} %add_sqrt_fusion), kind=kLoop, calls=%fused_computation.7 | loop fusion | flops 69120 | bytes 92240 | tf_op jit(solution)/shard_map/convert_element_type | solution.py:248
  2.6 3.0 %collective-permute-start = (bf16[20,1152]{1,0:T(8,128)(2,1)S(1)}, bf16[20,1152]{1,0:T(8,128)(2,1)S(1)}, u32[]{:S(2)}, u32[]{:S(2)}) collective-permute-start(bf16[20,1152]{1,0:T(8,128)(2,1)S(1)} %fusion.1), channel_id=1, source_target_pairs={{0,1},{1,0},{2,3},{3,2},{4,5},{5,4},{6,7},{7,6},{8,9},{9,8},{10,11... | collective-permute-start | bytes 138248 | tf_op jit(solution)/shard_map/ppermute | solution.py:107
  5.7 0.1 collective-permute-start.1
  5.7 0.8 %fusion.2 = (s32[20]{0:T(128)S(1)}, s32[20]{0:T(128)S(1)}) fusion(s32[40]{0:T(128)} %param.9), kind=kLoop, calls=%fused_computation.17 | loop fusion | bytes 320 | tf_op jit(solution)/shard_map/jit(_roll_static)/slice | solution.py:249
  6.5 0.7 %broadcast_select_fusion = s32[40]{0:T(128)S(1)} fusion(s32[40]{0:T(128)} %param.9, pred[]{:T(512)S(6)} %eq.5, s32[20]{0:T(128)S(1)} %get-tuple-element.32, s32[20]{0:T(128)S(1)} %get-tuple-element.31), kind=kLoop, calls=%fused_computation.13 | loop fusion | flops 80 | bytes 481 | tf_op jit(solution)/shard_map/jit(_where)/select_n | solution.py:249
  7.3 1.9 %collective-permute-start.9 = (s32[40]{0:T(128)S(1)}, s32[40]{0:T(128)S(1)}, u32[]{:S(2)}, u32[]{:S(2)}) collective-permute-start(s32[40]{0:T(128)S(1)} %broadcast_select_fusion), channel_id=1, source_target_pairs={{0,4},{1,5},{2,6},{3,7},{4,0},{5,1},{6,2},{7,3},{8,12},{9,13},{10,... | collective-permute-start | bytes 488 | tf_op jit(solution)/shard_map/ppermute | solution.py:107
  9.2 1.6 %collective-permute-done.9 = s32[40]{0:T(128)S(1)} collective-permute-done((s32[40]{0:T(128)S(1)}, s32[40]{0:T(128)S(1)}, u32[]{:S(2)}, u32[]{:S(2)}) %collective-permute-start.9) | collective-permute-done | bytes 192 | tf_op jit(solution)/shard_map/ppermute | solution.py:107
  10.8 0.1 pad_add_fusion.3
  10.9 0.0 collective-permute-done
  10.9 3.1 %collective-permute-start.11 = (s32[80]{0:T(128)S(1)}, s32[80]{0:T(128)S(1)}, u32[]{:S(2)}, u32[]{:S(2)}) collective-permute-start(s32[80]{0:T(128)S(1)} %pad_add_fusion.3), channel_id=1, source_target_pairs={{0,16},{1,17},{2,18},{3,19},{4,20},{5,21},{6,22},{7,23},{8,24},{9,... | collective-permute-start | bytes 968 | tf_op jit(solution)/shard_map/ppermute | solution.py:107
  14.0 0.0 collective-permute-done.1
  14.0 0.8 %pad_maximum_fusion.5 = bf16[40,1152]{1,0:T(8,128)(2,1)S(1)} fusion(bf16[20,1152]{1,0:T(8,128)(2,1)S(1)} %collective-permute-done.1, bf16[20,1152]{1,0:T(8,128)(2,1)} %param.7), kind=kLoop, calls=%fused_computation.9 | loop fusion | flops 184320 | bytes 184320 | tf_op jit(solution)/shard_map/concatenate | solution.py:235
  14.8 0.1 collective-permute-start.4
  14.9 1.8 %collective-permute-start.10 = (bf16[40,1152]{1,0:T(8,128)(2,1)S(1)}, bf16[40,1152]{1,0:T(8,128)(2,1)S(1)}, u32[]{:S(2)}, u32[]{:S(2)}) collective-permute-start(bf16[40,1152]{1,0:T(8,128)(2,1)S(1)} %pad_maximum_fusion.4.images), channel_id=1, source_target_pairs={{0,4},{1,5},{2,6},{3,7},{4,0},{5,1},{6,2},{7,3},{8,12},{9,13},{10,... | collective-permute-start | bytes 276488 | tf_op jit(solution)/shard_map/ppermute | solution.py:107
  16.7 0.0 collective-permute-done.11
  16.7 0.1 pad_add_fusion.2
  16.8 3.5 %collective-permute-done.4 = bf16[40,1152]{1,0:T(8,128)(2,1)S(1)} collective-permute-done((bf16[40,1152]{1,0:T(8,128)(2,1)S(1)}, bf16[40,1152]{1,0:T(8,128)(2,1)S(1)}, u32[]{:S(2)}, u32[]{:S(2)}) %collective-permute-start.4) | collective-permute-done | bytes 92192 | tf_op jit(solution)/shard_map/ppermute | solution.py:107
  20.4 0.8 %pad_maximum_fusion.2 = bf16[80,1152]{1,0:T(8,128)(2,1)S(1)} fusion(bf16[40,1152]{1,0:T(8,128)(2,1)S(1)} %collective-permute-done.4, bf16[20,1152]{1,0:T(8,128)(2,1)S(1)} %collective-permute-done.1, bf16[20,1152]{1,0:T(8,128)(2,1)} %param.7), kind=kLoop, calls=%fused_computation.2 | loop fusion | flops 552960 | bytes 368640 | tf_op jit(solution)/shard_map/concatenate | solution.py:235
  21.2 1.6 %collective-permute-start.5 = (bf16[80,1152]{1,0:T(8,128)(2,1)S(1)}, bf16[80,1152]{1,0:T(8,128)(2,1)S(1)}, u32[]{:S(2)}, u32[]{:S(2)}) collective-permute-start(bf16[80,1152]{1,0:T(8,128)(2,1)S(1)} %pad_maximum_fusion.2), channel_id=1, source_target_pairs={{0,8},{1,9},{2,10},{3,11},{4,12},{5,13},{6,14},{7,15},{8,0},{9,1},... | collective-permute-start | bytes 552968 | tf_op jit(solution)/shard_map/ppermute | solution.py:107
  22.8 0.0 collective-permute-done.10
  22.9 0.5 collective-permute-start.13
  23.4 1.1 %constant_dynamic-slice_fusion = bf16[288,1152]{1,0:T(8,128)(2,1)S(1)} fusion(bf16[576,1152]{1,0:T(8,128)(2,1)} %rest_0_.1, s32[]{:T(128)S(6)} %select_n.21), kind=kLoop, calls=%fused_computation.16 | loop fusion | bytes 1327108 | tf_op jit(solution)/shard_map/dynamic_slice | solution.py:238
  24.5 0.9 %collective-permute-start.2 = (bf16[288,1152]{1,0:T(8,128)(2,1)S(1)}, bf16[288,1152]{1,0:T(8,128)(2,1)S(1)}, u32[]{:S(2)}, u32[]{:S(2)}) collective-permute-start(bf16[288,1152]{1,0:T(8,128)(2,1)S(1)} %constant_dynamic-slice_fusion), channel_id=1, source_target_pairs={{0,1},{1,0},{2,3},{3,2},{4,5},{5,4},{6,7},{7,6},{8,9},{9,8},{10,11... | collective-permute-start | bytes 1990664 | tf_op jit(solution)/shard_map/ppermute | solution.py:107
  25.5 0.8 %collective-permute-start.12 = (bf16[80,1152]{1,0:T(8,128)(2,1)S(1)}, bf16[80,1152]{1,0:T(8,128)(2,1)S(1)}, u32[]{:S(2)}, u32[]{:S(2)}) collective-permute-start(bf16[80,1152]{1,0:T(8,128)(2,1)S(1)} %pad_maximum_fusion.3), channel_id=1, source_target_pairs={{0,16},{1,17},{2,18},{3,19},{4,20},{5,21},{6,22},{7,23},{8,24},{9,... | collective-permute-start | bytes 552968 | tf_op jit(solution)/shard_map/ppermute | solution.py:107
  26.2 2.3 %collective-permute-done.13 = s32[160]{0:T(256)S(1)} collective-permute-done((s32[160]{0:T(256)S(1)}, s32[160]{0:T(256)S(1)}, u32[]{:S(2)}, u32[]{:S(2)}) %collective-permute-start.13) | collective-permute-done | bytes 672 | tf_op jit(solution)/shard_map/ppermute | solution.py:107
  28.5 0.1 pad_add_fusion.1
  28.6 0.0 collective-permute-done.5
  28.6 0.0 copy-done.3
  28.6 1.9 %collective-permute-start.6 = (bf16[160,1152]{1,0:T(8,128)(2,1)S(1)}, bf16[160,1152]{1,0:T(8,128)(2,1)}, u32[]{:S(2)}, u32[]{:S(2)}) collective-permute-start(bf16[160,1152]{1,0:T(8,128)(2,1)S(1)} %pad_maximum_fusion.rest_3_), channel_id=1, source_target_pairs={{0,4},{1,5},{2,6},{3,7},{4,0},{5,1},{6,2},{7,3},{8,12},{9,13},{10,... | collective-permute-start | bytes 1105928 | tf_op jit(solution)/shard_map/ppermute | solution.py:107
  30.5 3.3 %collective-permute-done.12 = bf16[80,1152]{1,0:T(8,128)(2,1)S(1)} collective-permute-done((bf16[80,1152]{1,0:T(8,128)(2,1)S(1)}, bf16[80,1152]{1,0:T(8,128)(2,1)S(1)}, u32[]{:S(2)}, u32[]{:S(2)}) %collective-permute-start.12) | collective-permute-done | bytes 184352 | tf_op jit(solution)/shard_map/ppermute | solution.py:107
  33.8 0.8 %collective-permute-start.15 = (bf16[160,1152]{1,0:T(8,128)(2,1)S(1)}, bf16[160,1152]{1,0:T(8,128)(2,1)}, u32[]{:S(2)}, u32[]{:S(2)}) collective-permute-start(bf16[160,1152]{1,0:T(8,128)(2,1)S(1)} %pad_maximum_fusion.1.rest_0_), channel_id=1, source_target_pairs={{0,8},{1,9},{2,10},{3,11},{4,12},{5,13},{6,14},{7,15},{8,0},{9,1},... | collective-permute-start | bytes 1105928 | tf_op jit(solution)/shard_map/ppermute | solution.py:107
  34.6 3.2 %collective-permute-done.2.rest_1_ = bf16[288,1152]{1,0:T(8,128)(2,1)S(1)} collective-permute-done((bf16[288,1152]{1,0:T(8,128)(2,1)S(1)}, bf16[288,1152]{1,0:T(8,128)(2,1)S(1)}, u32[]{:S(2)}, u32[]{:S(2)}) %collective-permute-start.2) | collective-permute-done | bytes 663584 | tf_op jit(solution)/shard_map/ppermute | solution.py:107
  37.8 0.0 collective-permute-start.3
  37.8 0.5 collective-permute-start.14
  38.4 0.0 collective-permute-start.7
  38.4 0.0 collective-permute-done.6.rest_4_
  38.4 0.5 collective-permute-start.8
  38.9 1.1 %collective-permute-done.14 = s32[320]{0:T(512)S(1)} collective-permute-done((s32[320]{0:T(512)S(1)}, s32[320]{0:T(512)S(1)}, u32[]{:S(2)}, u32[]{:S(2)}) %collective-permute-start.14) | collective-permute-done | bytes 1312 | tf_op jit(solution)/shard_map/ppermute | solution.py:107
  40.0 0.1 collective-permute-start.16
  40.1 1.4 %collective-permute-done.15.rest_1_ = bf16[160,1152]{1,0:T(8,128)(2,1)} collective-permute-done((bf16[160,1152]{1,0:T(8,128)(2,1)S(1)}, bf16[160,1152]{1,0:T(8,128)(2,1)}, u32[]{:S(2)}, u32[]{:S(2)}) %collective-permute-start.15) | collective-permute-done | bytes 368672 | tf_op jit(solution)/shard_map/ppermute | solution.py:107
  41.5 0.0 collective-permute-start.17
  42.8 0.7 %copy.9.match = s32[40,1]{1,0:T(8,128)} copy(s32[40,1]{0,1:T(1,128)S(1)} %bitcast.1) | data formatting | bytes 320 | tf_op jit(solution)/shard_map/broadcast_in_dim | solution.py:280
  43.5 0.1 pad_add_fusion
  43.6 0.0 collective-permute-done.7.rest_5_
  43.6 0.0 collective-permute-done.8.rest_6_
  43.6 0.0 collective-permute-done.3.rest_2_
  43.6 0.0 copy-done.1
  43.6 0.0 copy-done
  43.6 0.0 copy-start.2
  43.6 0.7 %copy-done.2 = s32[40,1]{1,0:T(8,128)S(1)} copy-done((s32[40,1]{1,0:T(8,128)S(1)}, s32[40,1]{1,0:T(8,128)}, u32[]{:S(2)}) %copy-start.2) | copy-done | bytes 184
  44.3 6.7 %texts.1 = (bf16[640,1152]{1,0:T(8,128)(2,1)S(1)}, f32[640,1152]{1,0:T(8,128)S(1)}, bf16[576,640]{1,0:T(8,128)(2,1)S(1)}, bf16[1152,1152]{1,0:T(8,128)(2,1)S(1)}, f32[20,1152]{1,0:T(8,128)}) custom-call(f32[1]{0:T(128)S(6)} %copy.10.sharpness, f32[1]{0:T(128)S(6)} %copy.11.shift, bf16[20,1152]{1,0:T(8,128)(2,1)S(1)} %copy-done.1, ...), custom_call_target="tpu_custom_call" | custom-call | tf_op jit(solution)/shard_map/texts/pallas_call | solution.py:261
  51.0 0.0 collective-permute-done.16.rest_2_
  51.0 0.0 collective-permute-done.17.rest_3_
  51.0 7.9 %pairs.1 = (f32[20,1152]{1,0:T(8,128)}, f32[576,1152]{1,0:T(8,128)}) custom-call(f32[1]{0:T(128)S(6)} %copy.10.sharpness, f32[1]{0:T(128)S(6)} %copy.11.shift, s32[1,640]{1,0:T(1,128)S(1)} %broadcast_in_dim.8.match, bf16[640,1152]{1,0:T(8,128)(2,1)S(1)} %get-tuple-element.24.zt, f32[640,1152]{1,0:T(8,128)S(1)} %get-tuple-element.25.projected, ...), custom_call_target="tpu_custom_call" | custom-call | tf_op jit(solution)/shard_map/pairs/pallas_call | solution.py:286
  (6 shorter events, 0.1 us)
Async XLA Ops:
  0.6 42.9 %copy-start.1 = (bf16[20,1152]{1,0:T(8,128)(2,1)S(1)}, bf16[20,1152]{1,0:T(8,128)(2,1)}, u32[]{:S(2)}) copy-start(bf16[20,1152]{1,0:T(8,128)(2,1)} %image.1) | copy-start | bytes 138244
  0.6 27.9 %copy-start.3 = (bf16[20,1152]{1,0:T(8,128)(2,1)S(1)}, bf16[20,1152]{1,0:T(8,128)(2,1)}, u32[]{:S(2)}) copy-start(bf16[20,1152]{1,0:T(8,128)(2,1)} %param.7) | copy-start | bytes 138244
  0.7 42.9 %copy-start = (bf16[576,1152]{1,0:T(8,128)(2,1)S(1)}, bf16[576,1152]{1,0:T(8,128)(2,1)}, u32[]{:S(2)}) copy-start(bf16[576,1152]{1,0:T(8,128)(2,1)} %rest_0_.1) | copy-start | bytes 3981316
  2.6 8.3 %collective-permute-start = (bf16[20,1152]{1,0:T(8,128)(2,1)S(1)}, bf16[20,1152]{1,0:T(8,128)(2,1)S(1)}, u32[]{:S(2)}, u32[]{:S(2)}) collective-permute-start(bf16[20,1152]{1,0:T(8,128)(2,1)S(1)} %fusion.1), channel_id=1, source_target_pairs={{0,1},{1,0},{2,3},{3,2},{4,5},{5,4},{6,7},{7,6},{8,9},{9,8},{10,11... | collective-permute-start | bytes 138248 | tf_op jit(solution)/shard_map/ppermute | solution.py:107
  5.7 8.3 %collective-permute-start.1 = (bf16[20,1152]{1,0:T(8,128)(2,1)}, bf16[20,1152]{1,0:T(8,128)(2,1)S(1)}, u32[]{:S(2)}, u32[]{:S(2)}) collective-permute-start(bf16[20,1152]{1,0:T(8,128)(2,1)} %param.7), channel_id=1, source_target_pairs={{0,1},{1,0},{2,3},{3,2},{4,5},{5,4},{6,7},{7,6},{8,9},{9,8},{10,11... | collective-permute-start | bytes 138248 | tf_op jit(solution)/shard_map/ppermute | solution.py:107
  7.3 3.5 %collective-permute-start.9 = (s32[40]{0:T(128)S(1)}, s32[40]{0:T(128)S(1)}, u32[]{:S(2)}, u32[]{:S(2)}) collective-permute-start(s32[40]{0:T(128)S(1)} %broadcast_select_fusion), channel_id=1, source_target_pairs={{0,4},{1,5},{2,6},{3,7},{4,0},{5,1},{6,2},{7,3},{8,12},{9,13},{10,... | collective-permute-start | bytes 488 | tf_op jit(solution)/shard_map/ppermute | solution.py:107
  10.9 5.8 %collective-permute-start.11 = (s32[80]{0:T(128)S(1)}, s32[80]{0:T(128)S(1)}, u32[]{:S(2)}, u32[]{:S(2)}) collective-permute-start(s32[80]{0:T(128)S(1)} %pad_add_fusion.3), channel_id=1, source_target_pairs={{0,16},{1,17},{2,18},{3,19},{4,20},{5,21},{6,22},{7,23},{8,24},{9,... | collective-permute-start | bytes 968 | tf_op jit(solution)/shard_map/ppermute | solution.py:107
  14.8 5.5 %collective-permute-start.4 = (bf16[40,1152]{1,0:T(8,128)(2,1)S(1)}, bf16[40,1152]{1,0:T(8,128)(2,1)S(1)}, u32[]{:S(2)}, u32[]{:S(2)}) collective-permute-start(bf16[40,1152]{1,0:T(8,128)(2,1)S(1)} %pad_maximum_fusion.5), channel_id=1, source_target_pairs={{0,16},{1,17},{2,18},{3,19},{4,20},{5,21},{6,22},{7,23},{8,24},{9,... | collective-permute-start | bytes 276488 | tf_op jit(solution)/shard_map/ppermute | solution.py:107
  14.9 7.9 %collective-permute-start.10 = (bf16[40,1152]{1,0:T(8,128)(2,1)S(1)}, bf16[40,1152]{1,0:T(8,128)(2,1)S(1)}, u32[]{:S(2)}, u32[]{:S(2)}) collective-permute-start(bf16[40,1152]{1,0:T(8,128)(2,1)S(1)} %pad_maximum_fusion.4.images), channel_id=1, source_target_pairs={{0,4},{1,5},{2,6},{3,7},{4,0},{5,1},{6,2},{7,3},{8,12},{9,13},{10,... | collective-permute-start | bytes 276488 | tf_op jit(solution)/shard_map/ppermute | solution.py:107
  21.2 7.4 %collective-permute-start.5 = (bf16[80,1152]{1,0:T(8,128)(2,1)S(1)}, bf16[80,1152]{1,0:T(8,128)(2,1)S(1)}, u32[]{:S(2)}, u32[]{:S(2)}) collective-permute-start(bf16[80,1152]{1,0:T(8,128)(2,1)S(1)} %pad_maximum_fusion.2), channel_id=1, source_target_pairs={{0,8},{1,9},{2,10},{3,11},{4,12},{5,13},{6,14},{7,15},{8,0},{9,1},... | collective-permute-start | bytes 552968 | tf_op jit(solution)/shard_map/ppermute | solution.py:107
  22.9 5.6 %collective-permute-start.13 = (s32[160]{0:T(256)S(1)}, s32[160]{0:T(256)S(1)}, u32[]{:S(2)}, u32[]{:S(2)}) collective-permute-start(s32[160]{0:T(256)S(1)} %pad_add_fusion.2), channel_id=1, source_target_pairs={{0,8},{1,9},{2,10},{3,11},{4,12},{5,13},{6,14},{7,15},{8,0},{9,1},... | collective-permute-start | bytes 1928 | tf_op jit(solution)/shard_map/ppermute | solution.py:107
  24.5 13.3 %collective-permute-start.2 = (bf16[288,1152]{1,0:T(8,128)(2,1)S(1)}, bf16[288,1152]{1,0:T(8,128)(2,1)S(1)}, u32[]{:S(2)}, u32[]{:S(2)}) collective-permute-start(bf16[288,1152]{1,0:T(8,128)(2,1)S(1)} %constant_dynamic-slice_fusion), channel_id=1, source_target_pairs={{0,1},{1,0},{2,3},{3,2},{4,5},{5,4},{6,7},{7,6},{8,9},{9,8},{10,11... | collective-permute-start | bytes 1990664 | tf_op jit(solution)/shard_map/ppermute | solution.py:107
  25.5 8.3 %collective-permute-start.12 = (bf16[80,1152]{1,0:T(8,128)(2,1)S(1)}, bf16[80,1152]{1,0:T(8,128)(2,1)S(1)}, u32[]{:S(2)}, u32[]{:S(2)}) collective-permute-start(bf16[80,1152]{1,0:T(8,128)(2,1)S(1)} %pad_maximum_fusion.3), channel_id=1, source_target_pairs={{0,16},{1,17},{2,18},{3,19},{4,20},{5,21},{6,22},{7,23},{8,24},{9,... | collective-permute-start | bytes 552968 | tf_op jit(solution)/shard_map/ppermute | solution.py:107
  28.6 9.7 %collective-permute-start.6 = (bf16[160,1152]{1,0:T(8,128)(2,1)S(1)}, bf16[160,1152]{1,0:T(8,128)(2,1)}, u32[]{:S(2)}, u32[]{:S(2)}) collective-permute-start(bf16[160,1152]{1,0:T(8,128)(2,1)S(1)} %pad_maximum_fusion.rest_3_), channel_id=1, source_target_pairs={{0,4},{1,5},{2,6},{3,7},{4,0},{5,1},{6,2},{7,3},{8,12},{9,13},{10,... | collective-permute-start | bytes 1105928 | tf_op jit(solution)/shard_map/ppermute | solution.py:107
  33.8 7.7 %collective-permute-start.15 = (bf16[160,1152]{1,0:T(8,128)(2,1)S(1)}, bf16[160,1152]{1,0:T(8,128)(2,1)}, u32[]{:S(2)}, u32[]{:S(2)}) collective-permute-start(bf16[160,1152]{1,0:T(8,128)(2,1)S(1)} %pad_maximum_fusion.1.rest_0_), channel_id=1, source_target_pairs={{0,8},{1,9},{2,10},{3,11},{4,12},{5,13},{6,14},{7,15},{8,0},{9,1},... | collective-permute-start | bytes 1105928 | tf_op jit(solution)/shard_map/ppermute | solution.py:107
  37.8 5.7 %collective-permute-start.3 = (bf16[288,1152]{1,0:T(8,128)(2,1)S(1)}, bf16[288,1152]{1,0:T(8,128)(2,1)S(1)}, u32[]{:S(2)}, u32[]{:S(2)}) collective-permute-start(bf16[288,1152]{1,0:T(8,128)(2,1)S(1)} %collective-permute-done.2.rest_1_), channel_id=1, source_target_pairs={{0,2},{1,3},{2,0},{3,1},{4,6},{5,7},{6,4},{7,5},{8,10},{9,11},{10,... | collective-permute-start | bytes 1990664 | tf_op jit(solution)/shard_map/ppermute | solution.py:107
  37.8 2.1 %collective-permute-start.14 = (s32[320]{0:T(512)S(1)}, s32[320]{0:T(512)S(1)}, u32[]{:S(2)}, u32[]{:S(2)}) collective-permute-start(s32[320]{0:T(512)S(1)} %pad_add_fusion.1), channel_id=1, source_target_pairs={{0,2},{1,3},{2,0},{3,1},{4,6},{5,7},{6,4},{7,5},{8,10},{9,11},{10,... | collective-permute-start | bytes 3848 | tf_op jit(solution)/shard_map/ppermute | solution.py:107
  38.4 5.2 %collective-permute-start.7 = (bf16[160,1152]{1,0:T(8,128)(2,1)S(1)}, bf16[160,1152]{1,0:T(8,128)(2,1)}, u32[]{:S(2)}, u32[]{:S(2)}) collective-permute-start(bf16[160,1152]{1,0:T(8,128)(2,1)S(1)} %pad_maximum_fusion.rest_3_), channel_id=1, source_target_pairs={{0,2},{1,3},{2,0},{3,1},{4,6},{5,7},{6,4},{7,5},{8,10},{9,11},{10,... | collective-permute-start | bytes 1105928 | tf_op jit(solution)/shard_map/ppermute | solution.py:107
  38.4 5.2 %collective-permute-start.8 = (bf16[160,1152]{1,0:T(8,128)(2,1)}, bf16[160,1152]{1,0:T(8,128)(2,1)}, u32[]{:S(2)}, u32[]{:S(2)}) collective-permute-start(bf16[160,1152]{1,0:T(8,128)(2,1)} %collective-permute-done.6.rest_4_), channel_id=1, source_target_pairs={{0,2},{1,3},{2,0},{3,1},{4,6},{5,7},{6,4},{7,5},{8,10},{9,11},{10,... | collective-permute-start | bytes 1105928 | tf_op jit(solution)/shard_map/ppermute | solution.py:107
  40.0 11.1 %collective-permute-start.16 = (bf16[160,1152]{1,0:T(8,128)(2,1)S(1)}, bf16[160,1152]{1,0:T(8,128)(2,1)}, u32[]{:S(2)}, u32[]{:S(2)}) collective-permute-start(bf16[160,1152]{1,0:T(8,128)(2,1)S(1)} %pad_maximum_fusion.1.rest_0_), channel_id=1, source_target_pairs={{0,2},{1,3},{2,0},{3,1},{4,6},{5,7},{6,4},{7,5},{8,10},{9,11},{10,... | collective-permute-start | bytes 1105928 | tf_op jit(solution)/shard_map/ppermute | solution.py:107
  41.5 9.5 %collective-permute-start.17 = (bf16[160,1152]{1,0:T(8,128)(2,1)}, bf16[160,1152]{1,0:T(8,128)(2,1)}, u32[]{:S(2)}, u32[]{:S(2)}) collective-permute-start(bf16[160,1152]{1,0:T(8,128)(2,1)} %collective-permute-done.15.rest_1_), channel_id=1, source_target_pairs={{0,2},{1,3},{2,0},{3,1},{4,6},{5,7},{6,4},{7,5},{8,10},{9,11},{10,... | collective-permute-start | bytes 1105928 | tf_op jit(solution)/shard_map/ppermute | solution.py:107
  43.6 0.7 %copy-start.2 = (s32[40,1]{1,0:T(8,128)S(1)}, s32[40,1]{1,0:T(8,128)}, u32[]{:S(2)}) copy-start(s32[40,1]{1,0:T(8,128)} %copy.9.match) | copy-start | bytes 484
